TPU v7x, 768 devices: a whole 4x8x12 slice. The times are simulated.
768 devices in a mesh: ver: 2 (over z_hi), fsdp: 48 (over y, z_lo), tp: 8 (over x, core).
Axes of the slice: x: 4, y: 8, z: 12 (z_hi: 2, z_lo: 6; z = z_hi * 6 + z_lo), core: 2. Of those that a mesh axis runs over, the one named last changes fastest.
Arguments:
- train_acts: bfloat16 [2, 96, 128, 8192], P('ver', 'fsdp', None, 'tp'), may hold values from -6 to 6
- train_grads: bfloat16 [2, 96, 128, 24576], P('ver', 'fsdp', None, 'tp'), may hold values from -6 to 6
- query_acts: bfloat16 [2, 48, 128, 8192], P('ver', 'fsdp', None, 'tp'), may hold values from -6 to 6
- query_grads: bfloat16 [2, 48, 128, 24576], P('ver', 'fsdp', None, 'tp'), may hold values from -6 to 6
- proj_in: bfloat16 [64, 8192], P(None, 'tp'), may hold values from -0.0625 to 0.0625
- proj_out: bfloat16 [64, 24576], P(None, ('tp', 'fsdp')), may hold values from -0.0390625 to 0.0390625
- step_sizes: float32 [2], P('ver'), may hold values from 0.5 to 2
Outputs:
- influence: float32 [96, 48], P('fsdp')
All inputs are finite; a program needn't handle non-finite values.
Results may differ from a plain program's by a relative error of at most 0.0003.
Values may be sent and summed in bfloat16 or wider, within the bound.
A program may use at most 32 MiB of HBM per device.

v0:
```python
import jax
import jax.numpy as jnp
from jax import lax
from jax.sharding import PartitionSpec as P


def project_inputs(acts, proj_in):
    flattened = acts.reshape(-1, acts.shape[-1])
    return jnp.dot(flattened, proj_in.T, preferred_element_type=jnp.float32)


def body(train_acts, train_grads, query_acts, query_grads, proj_in, proj_out, step_sizes):
    rank = proj_in.shape[0]
    seq_len = train_acts.shape[2]
    train_count = train_acts.shape[1]
    query_count = query_acts.shape[1]
    examples = train_count + query_count
    train_flat = train_grads.reshape(-1, train_grads.shape[-1])
    query_flat = query_grads.reshape(-1, query_grads.shape[-1])
    segment = lax.all_gather(proj_out, "fsdp", axis=1, tiled=True)
    train_out = jnp.dot(train_flat, segment.T, preferred_element_type=jnp.float32)
    query_out = jnp.dot(query_flat, segment.T, preferred_element_type=jnp.float32)
    train_in = project_inputs(train_acts, proj_in)
    query_in = project_inputs(query_acts, proj_in)
    inputs_all = jnp.concatenate([train_in, query_in], 0).reshape(examples, seq_len, rank)
    outputs_all = jnp.concatenate([train_out, query_out], 0).reshape(examples, seq_len, rank)
    step_size = step_sizes[0]
    inputs_sum, outputs_sum = lax.psum((inputs_all, outputs_all), "tp")
    grads_all = (
        jnp.einsum("nsa,nsb->nab", inputs_sum, outputs_sum, precision=lax.Precision.HIGHEST)
        / seq_len
    )
    train_part = grads_all[:train_count]
    query_part = grads_all[train_count:]
    gathered = lax.all_gather(query_part, "fsdp", axis=0, tiled=True)
    gram_part = (
        jnp.dot(
            train_part.reshape(train_count, -1),
            gathered.reshape(gathered.shape[0], -1).T,
            precision=lax.Precision.HIGHEST,
        )
        * step_size
    )
    return lax.psum(gram_part, "ver")


def solution(mesh):
    in_specs = (
        P("ver", "fsdp", None, "tp"),
        P("ver", "fsdp", None, "tp"),
        P("ver", "fsdp", None, "tp"),
        P("ver", "fsdp", None, "tp"),
        P(None, "tp"),
        P(None, ("tp", "fsdp")),
        P("ver"),
    )
    out_specs = P("fsdp", None)
    return jax.shard_map(body, mesh=mesh, in_specs=in_specs, out_specs=out_specs, check_vma=False)
```

profile of v0, /device:TPU:6, one launch (start us, length us, event | category | flops | bytes accessed | tf_op | source)
XLA Modules:
  0.0 440.3 jit_solution(2653645866756808885)
XLA Ops:
  6.5 0.0 copy-start
  6.5 0.0 copy-start.1
  6.5 0.0 all-reduce.3.cloned.1.call-start
  6.5 0.9 copy.17
  7.5 1.2 fusion.10
  8.7 1.3 fusion.13
  10.0 165.5 %all_gather.6 = bf16[64,3072]{0,1:T(8,128)(2,1)S(1)} all-gather(bf16[64,64]{0,1:T(8,128)(2,1)S(1)} %copy.17), channel_id=1, replica_groups=mesh['ver'=2,'fsdp'=48,'tp'=8] {'fsdp'}, dimensions={1}, use_global_device_ids=true | all-gather | bytes 401408 | tf_op jit(solution)/shard_map/all_gather | solution.py:20
  175.5 0.0 copy-done.1
  175.5 0.5 fusion.8
  176.0 0.0 copy-done
  176.0 0.6 fusion.14
  176.6 0.7 copy_bitcast_fusion
  177.3 0.0 all-reduce.3.cloned.1.call-update
  178.0 71.0 %all-reduce.3.cloned.1.call-done = (f32[3,128,64]{1,2,0:T(8,128)}, f32[3,128,64]{1,2,0:T(8,128)}) async-done(((f32[3,128,64]{1,2,0:T(8,128)}, f32[3,128,64]{1,2,0:T(8,128)}), (f32[3,128,64]{1,2,0:T(8,128)}, f32[3,128,64]{1,2,0:T(8,128)})) %all-reduce.3.cloned.1.call-update) | async-done | bytes 196624 | tf_op jit(solution)/shard_map/psum | solution.py:28
  249.0 1.2 convolution_multiply_fusion
  250.3 169.3 %all_gather.7 = f32[48,64,64]{2,1,0:T(8,128)S(1)} all-gather(f32[1,64,64]{2,1,0:T(8,128)S(1)} %slice.9), channel_id=1, replica_groups=mesh['ver'=2,'fsdp'=48,'tp'=8] {'fsdp'}, dimensions={0}, use_global_device_ids=true | all-gather | bytes 802816 | tf_op jit(solution)/shard_map/all_gather | solution.py:35
  419.5 2.1 fusion.5
  421.6 11.8 %psum.23 = f32[2,48]{1,0:T(2,128)} all-reduce(f32[2,48]{1,0:T(2,128)S(1)} %fusion.5), channel_id=1, replica_groups=mesh['ver'=2,'fsdp'=48,'tp'=8] {'ver'}, use_global_device_ids=true, to_apply=%region_2.0 | all-reduce | flops 96 | bytes 768 | tf_op jit(solution)/shard_map/psum | solution.py:44
  (2 shorter events, 0.0 us)
Async XLA Ops:
  6.5 169.4 %copy-start = (bf16[1,2,128,3072]{3,2,1,0:T(8,128)(2,1)S(1)}, bf16[1,2,128,3072]{3,2,1,0:T(8,128)(2,1)}, u32[]{:S(2)}) copy-start(bf16[1,2,128,3072]{3,2,1,0:T(8,128)(2,1)} %param.8) | copy-start | bytes 4718596
  6.5 169.0 %copy-start.1 = (bf16[1,1,128,3072]{3,2,1,0:T(8,128)(2,1)S(1)}, bf16[1,1,128,3072]{3,2,1,0:T(8,128)(2,1)}, u32[]{:S(2)}) copy-start(bf16[1,1,128,3072]{3,2,1,0:T(8,128)(2,1)} %param.10) | copy-start | bytes 2359300
  6.5 242.5 %all-reduce.3.cloned.1.call-start = ((), (), s32[]{:S(2)}) async-start(), calls=%async_computation | async-start | bytes 393216 | tf_op jit(solution)/shard_map/psum | solution.py:28
Sparse Core Ops, SparseCore 0:
  177.4 71.4 all-reduce.2
where the time goes:
time: 441 us; the launch traced here: 440 us
  blocking collectives  347 us (79%)
  waiting for transfers between devices  71 us (16%)
  between operations  14.1 us (3%)
  matrix products  6.95 us (2%)
    all_gather x1, blocking collectives, body(): gathered = lax.all_gather(query_part, 'fsdp', axis=0, tiled=True)  169 us
    all_gather x1, blocking collectives, body(): segment = lax.all_gather(proj_out, 'fsdp', axis=1, tiled=True)  165 us
    psum x1, waiting for transfers between devices, body(): inputs_sum, outputs_sum = lax.psum((inputs_all, outputs_all), 'tp')  71 us
    psum x1, blocking collectives, body(): return lax.psum(gram_part, 'ver')  11.8 us
  transfers between devices with their start and end apart: 1, of which 1 were waited for; matrix products, arithmetic and copies ran while one was open for 0% of the time, Pallas kernels for 0%

commit v1 on v0

v1 whole, which is shorter than its diff:
```python
import functools

import jax
import jax.numpy as jnp
from jax import lax
from jax.experimental import pallas as pl
from jax.experimental.pallas import tpu as pltpu
from jax.sharding import PartitionSpec as P

NZ = 6
MESH = pl.DeviceIdType.MESH
F32 = jnp.float32
BF16 = jnp.bfloat16
NT = (((1,), (1,)), ((), ()))


def split(x):
    hi = x.astype(BF16)
    return hi, (x - hi.astype(F32)).astype(BF16)


def kernel(
    nver, ny, ntp,
    train_acts, train_grads, query_acts, query_grads, proj_in, proj_out, step,
    out,
    acts, grads, pin, pout, pbuf, at_part, at_recv, at_full, bsum, gp, grecv, zq, crow, dbuf,
    load_sem, pz_recv, pr_recv, pl_recv, p_send, ring_send,
    a_send, a_recv, ag_send, ag_recv, g_send, g_recv, z_send, z_recv, y_send, y_recv, d_send, d_recv,
):
    ver = lax.axis_index("ver")
    fsdp = lax.axis_index("fsdp")
    tp = lax.axis_index("tp")
    y, z = fsdp // NZ, fsdp % NZ
    half = NZ // 2
    trains, queries = train_acts.shape[1], query_acts.shape[1]
    count = trains + queries
    seq = train_acts.shape[2]
    tokens = count * seq

    def at_z(d):
        return {"fsdp": y * NZ + (z + d) % NZ}

    def at_y(d):
        return {"fsdp": ((y + d) % ny) * NZ + z}

    def at_tp(d):
        return {"tp": (tp + d) % ntp}

    def at_ver(v, d):
        return {"ver": (ver + v) % nver, "tp": (tp + d) % ntp}

    def push(src, dst, send, recv, where):
        copy = pltpu.make_async_remote_copy(
            src_ref=src, dst_ref=dst, send_sem=send, recv_sem=recv, device_id=where, device_id_type=MESH
        )
        copy.start()

    def wait(ref, sem):
        pltpu.make_async_copy(ref, ref, sem).wait()

    load_pout = pltpu.make_async_copy(proj_out, pout, load_sem.at[0])
    load_pout.start()
    barrier = pltpu.get_barrier_semaphore()
    partners = [at_y(d) for d in range(1, ny)] + [at_z(d) for d in range(1, NZ)] + [at_tp(d) for d in range(1, ntp)]
    partners += [at_ver(v, d) for v in range(1, nver) for d in range(ntp)]
    for where in partners:
        pl.semaphore_signal(barrier, inc=1, device_id=where, device_id_type=MESH)
    loads_a = [
        pltpu.make_async_copy(proj_in, pin, load_sem.at[1]),
        pltpu.make_async_copy(train_acts.at[0], acts.at[pl.ds(0, trains)], load_sem.at[2]),
        pltpu.make_async_copy(query_acts.at[0], acts.at[pl.ds(trains, queries)], load_sem.at[3]),
    ]
    loads_g = [
        pltpu.make_async_copy(train_grads.at[0], grads.at[pl.ds(0, trains)], load_sem.at[4]),
        pltpu.make_async_copy(query_grads.at[0], grads.at[pl.ds(trains, queries)], load_sem.at[5]),
    ]
    for load in loads_a + loads_g:
        load.start()

    load_pout.wait()
    own = pout[...].astype(F32)
    rank = own.shape[0]
    pbuf[y, z] = jnp.concatenate([own[: rank // 2], own[rank // 2 :]], axis=1).astype(BF16)

    pl.semaphore_wait(barrier, len(partners))
    for d in range(1, NZ):
        push(pbuf.at[y, z], pbuf.at[y, z], p_send, pz_recv.at[z], at_z(d))

    for load in loads_a:
        load.wait()
    a_part = lax.dot_general(pin[...], acts[...].reshape(tokens, -1), NT, preferred_element_type=F32)
    at_part[...] = a_part.reshape(at_part.shape)
    for d in range(1, ntp):
        push(at_part.at[(tp + d) % ntp], at_recv.at[d - 1], a_send, a_recv, at_tp(d))

    first = z // half
    chunks = (first, 1 - first)
    hops_right = (ny // 2, ny // 2 - 1)
    hops_left = (ny // 2 - 1, ny // 2)

    def send_right(s, k):
        row = (y + ny - s) % ny
        part = pbuf.at[row, pl.ds(chunks[k] * half, half)]
        push(part, part, ring_send, pr_recv.at[s * 2 + k], at_y(1))

    def send_left(s, k):
        row = (y + s) % ny
        part = pbuf.at[row, pl.ds(chunks[k] * half, half)]
        push(part, part, ring_send, pl_recv.at[s * 2 + k], at_y(ny - 1))

    lane = lax.broadcasted_iota(jnp.int32, (rank // 2, 2 * rank), 1)
    is_left = lane < rank

    def add_row(row, start):
        cols = []
        for p in range(half):
            even = pbuf[row, 2 * p].astype(F32)
            odd = pbuf[row, 2 * p + 1].astype(F32)
            low = jnp.where(is_left, even, pltpu.roll(odd, rank, 1)).astype(BF16)
            high = jnp.where(is_left, pltpu.roll(even, rank, 1), odd).astype(BF16)
            cols.append(jnp.concatenate([low, high, low, high], axis=0))
        width = NZ * rank
        g = grads[:, :, pl.ds(pl.multiple_of(row * width, 128), width)].reshape(tokens, width)
        term = lax.dot_general(g, jnp.concatenate(cols, axis=1), NT, preferred_element_type=F32)
        if start:
            bsum[...] = term
        else:
            bsum[...] += term

    one_block = pbuf.at[0, 0]
    one_chunk = pbuf.at[0, pl.ds(0, half)]
    for k in range(2):
        if k == 0:
            others = [first * half + (z % half + i) % half for i in range(1, half)]
        else:
            others = [(1 - first) * half + i for i in range(half)]
        for other in others:
            wait(one_block, pz_recv.at[other])
        if hops_right[k] > 0:
            send_right(0, k)
        if hops_left[k] > 0:
            send_left(0, k)
    for load in loads_g:
        load.wait()
    add_row(y, True)

    wait(at_recv, a_recv)
    mine = at_part[tp]
    for d in range(ntp - 1):
        mine = mine + at_recv[d]
    at_full[tp] = mine
    for d in range(1, ntp):
        push(at_full.at[tp], at_full.at[tp], ag_send, ag_recv, at_tp(d))

    for s in range(1, ny // 2 + 1):
        for k in range(2):
            if s - 1 < hops_right[k]:
                wait(one_chunk, pr_recv.at[(s - 1) * 2 + k])
                if s < hops_right[k]:
                    send_right(s, k)
            if s - 1 < hops_left[k]:
                wait(one_chunk, pl_recv.at[(s - 1) * 2 + k])
                if s < hops_left[k]:
                    send_left(s, k)
        add_row((y + ny - s) % ny, False)
        if s < ny // 2:
            add_row((y + s) % ny, False)

    wait(at_full.at[pl.ds(0, ntp - 1)], ag_recv)
    lanes2 = lax.broadcasted_iota(jnp.int32, (seq, 2 * rank), 1) < rank
    rows = rank // 2 // ntp
    for n in range(count):
        at = at_full[:, :, n * seq : (n + 1) * seq].reshape(rank, seq)
        a_hi, a_lo = split(jnp.concatenate([at[: rank // 2], at[rank // 2 :]], axis=1))
        b = bsum[n * seq : (n + 1) * seq, :]
        b_hi, b_lo = split(jnp.concatenate([jnp.where(lanes2, b, 0.0), jnp.where(lanes2, 0.0, b)], axis=0))
        both = jnp.dot(jnp.concatenate([a_hi, a_lo], axis=0), b_hi, preferred_element_type=F32)
        grad = both[: rank // 2] + (both[rank // 2 :] + jnp.dot(a_hi, b_lo, preferred_element_type=F32))
        for t in range(ntp):
            gp[t, n * rows : (n + 1) * rows, :] = grad[t * rows : (t + 1) * rows, :]
    for d in range(1, ntp):
        push(gp.at[(tp + d) % ntp], grecv.at[d - 1], g_send, g_recv, at_tp(d))
    wait(grecv, g_recv)
    grad = gp[tp]
    for d in range(ntp - 1):
        grad = grad + grecv[d]

    zq[z] = grad[trains * rows :, :]
    for d in range(1, NZ):
        push(zq.at[z], zq.at[z], z_send, z_recv, at_z(d))
    wait(zq.at[pl.ds(0, NZ - 1)], z_recv)
    for k in range(NZ):
        crow[y, k * rows : (k + 1) * rows, :] = zq[k]
    for d in range(1, ny):
        push(crow.at[y], crow.at[y], y_send, y_recv, at_y(d))
    wait(crow.at[pl.ds(0, ny - 1)], y_recv)

    wide = ny * NZ * rows
    q_hi, q_lo = split(crow[...].reshape(wide, 2 * rank))
    t_hi, t_lo = split(grad[: trains * rows, :])
    many = trains * rows
    both = lax.dot_general(jnp.concatenate([t_hi, t_lo], axis=0), q_hi, NT, preferred_element_type=F32)
    cross = both[:many] + (both[many:] + lax.dot_general(t_hi, q_lo, NT, preferred_element_type=F32))
    row_id = lax.broadcasted_iota(jnp.int32, (many, wide), 0) % rows
    col_id = lax.broadcasted_iota(jnp.int32, (many, wide), 1) % rows
    cross = jnp.where(row_id == col_id, cross, 0.0)
    c_hi, c_rest = cross.astype(BF16), cross
    c_rest = c_rest - c_hi.astype(F32)
    c_mid, c_lo = split(c_rest)
    pick_from = lax.broadcasted_iota(jnp.int32, (wide, 128), 0) // rows
    pick_to = lax.broadcasted_iota(jnp.int32, (wide, 128), 1)
    pick = jnp.where(pick_from == pick_to, 1.0, 0.0).astype(BF16)
    three = jnp.dot(jnp.concatenate([c_hi, c_mid, c_lo], axis=0), pick, preferred_element_type=F32)
    part = three[:many] + (three[many : 2 * many] + three[2 * many :])
    me = ver * ntp + tp
    dbuf[me] = part * (step[0] / (seq * seq))

    for v in reversed(range(nver)):
        for d in range(ntp):
            if v or d:
                push(dbuf.at[me], dbuf.at[me], d_send, d_recv, at_ver(v, d))
    wait(dbuf.at[pl.ds(0, nver * ntp - 1)], d_recv)
    total = dbuf[0]
    for i in range(1, nver * ntp):
        total = total + dbuf[i]
    width = out.shape[1]
    for n in range(trains):
        out[n : n + 1, :] = jnp.sum(total[n * rows : (n + 1) * rows, :], axis=0, keepdims=True)[:, :width]

    wait(pbuf.at[0, pl.ds(0, NZ - 1)], p_send)
    wait(pbuf.at[pl.ds(0, ny - 1)], ring_send)
    wait(at_recv, a_send)
    wait(at_recv, ag_send)
    wait(grecv, g_send)
    wait(zq.at[pl.ds(0, NZ - 1)], z_send)
    wait(crow.at[pl.ds(0, ny - 1)], y_send)
    wait(dbuf.at[pl.ds(0, nver * ntp - 1)], d_send)


def solution(mesh):
    nver, nfsdp, ntp = mesh.shape["ver"], mesh.shape["fsdp"], mesh.shape["tp"]
    ny = nfsdp // NZ

    def body(train_acts, train_grads, query_acts, query_grads, proj_in, proj_out, step_sizes):
        rank, din = proj_in.shape
        trains, queries = train_acts.shape[1], query_acts.shape[1]
        count, seq = trains + queries, train_acts.shape[2]
        tokens, dout = count * seq, train_grads.shape[3]
        arows = rank // ntp
        rows = rank // 2 // ntp
        dma = pltpu.SemaphoreType.DMA
        hbm = pl.BlockSpec(memory_space=pl.ANY)
        return pl.pallas_call(
            functools.partial(kernel, nver, ny, ntp),
            out_shape=jax.ShapeDtypeStruct((trains, nfsdp * queries), F32),
            in_specs=[hbm] * 6 + [pl.BlockSpec(memory_space=pltpu.SMEM)],
            out_specs=pl.BlockSpec(memory_space=pltpu.VMEM),
            scratch_shapes=[
                pltpu.VMEM((count, seq, din), BF16),
                pltpu.VMEM((count, seq, dout), BF16),
                pltpu.VMEM((rank, din), BF16),
                pltpu.VMEM(proj_out.shape, BF16),
                pltpu.VMEM((ny, NZ, rank // 2, 2 * proj_out.shape[1]), BF16),
                pltpu.VMEM((ntp, arows, tokens), F32),
                pltpu.VMEM((ntp - 1, arows, tokens), F32),
                pltpu.VMEM((ntp, arows, tokens), F32),
                pltpu.VMEM((tokens, 2 * rank), F32),
                pltpu.VMEM((ntp, count * rows, 2 * rank), F32),
                pltpu.VMEM((ntp - 1, count * rows, 2 * rank), F32),
                pltpu.VMEM((NZ, rows, 2 * rank), F32),
                pltpu.VMEM((ny, NZ * rows, 2 * rank), F32),
                pltpu.VMEM((nver * ntp, trains * rows, 128), F32),
                dma((6,)), dma((NZ,)), dma((ny,)), dma((ny,)), dma, dma,
                dma, dma, dma, dma, dma, dma, dma, dma, dma, dma, dma, dma,
            ],
            compiler_params=pltpu.CompilerParams(
                collective_id=0, has_side_effects=True, vmem_limit_bytes=40 * 1024 * 1024
            ),
        )(train_acts, train_grads, query_acts, query_grads, proj_in, proj_out, step_sizes)

    in_specs = (
        P("ver", "fsdp", None, "tp"),
        P("ver", "fsdp", None, "tp"),
        P("ver", "fsdp", None, "tp"),
        P("ver", "fsdp", None, "tp"),
        P(None, "tp"),
        P(None, ("tp", "fsdp")),
        P("ver"),
    )
    return jax.shard_map(body, mesh=mesh, in_specs=in_specs, out_specs=P("fsdp", None), check_vma=False)
```

time: 441 us -> 67.4 us (0.15)
  the two profiles are of different devices: /device:TPU:6 before, /device:TPU:1 now
where the time goes in v1:
time: 67.4 us; the launch traced here: 67.1 us
  Pallas kernels  59.7 us (89%)
  local copies, waits for them, and re-layouts  6.71 us (10%)
    pallas_call x1, Pallas kernels, body(): pl.pallas_call(functools.partial(kernel, nver, ny, ntp), out_shape=jax.Sh...  59.7 us
    unnamed x13, local copies, waits for them, and re-layouts  6.71 us

profile of v1, /device:TPU:1, one launch (start us, length us, event | category | flops | bytes accessed | tf_op | source)
XLA Modules:
  0.0 67.1 jit_solution(1244941911380927284)
XLA Ops:
  0.7 0.0 copy-start
  0.7 1.4 %copy-done = bf16[1,2,128,3072]{3,2,1,0:T(8,128)(2,1)S(1)} copy-done((bf16[1,2,128,3072]{3,2,1,0:T(8,128)(2,1)S(1)}, bf16[1,2,128,3072]{3,2,1,0:T(8,128)(2,1)}, u32[]{:S(2)}) %copy-start) | copy-done | bytes 1572888
  2.1 0.0 copy-start.1
  2.1 1.1 %copy-done.1 = bf16[1,1,128,3072]{3,2,1,0:T(8,128)(2,1)S(1)} copy-done((bf16[1,1,128,3072]{3,2,1,0:T(8,128)(2,1)S(1)}, bf16[1,1,128,3072]{3,2,1,0:T(8,128)(2,1)}, u32[]{:S(2)}) %copy-start.1) | copy-done | bytes 786456
  3.2 0.0 copy-start.2
  3.2 1.0 %copy-done.2 = bf16[1,2,128,1024]{3,2,1,0:T(8,128)(2,1)S(1)} copy-done((bf16[1,2,128,1024]{3,2,1,0:T(8,128)(2,1)S(1)}, bf16[1,2,128,1024]{3,2,1,0:T(8,128)(2,1)}, u32[]{:S(2)}) %copy-start.2) | copy-done | bytes 524312
  4.2 0.0 copy-start.3
  4.2 0.9 %copy-done.3 = bf16[1,1,128,1024]{3,2,1,0:T(8,128)(2,1)S(1)} copy-done((bf16[1,1,128,1024]{3,2,1,0:T(8,128)(2,1)S(1)}, bf16[1,1,128,1024]{3,2,1,0:T(8,128)(2,1)}, u32[]{:S(2)}) %copy-start.3) | copy-done | bytes 262168
  5.2 0.0 copy-start.4
  5.2 0.9 %copy-done.4 = bf16[64,1024]{1,0:T(8,128)(2,1)S(1)} copy-done((bf16[64,1024]{1,0:T(8,128)(2,1)S(1)}, bf16[64,1024]{1,0:T(8,128)(2,1)}, u32[]{:S(2)}) %copy-start.4) | copy-done | bytes 131096
  6.1 0.0 copy-start.5
  6.1 0.7 %copy-done.5 = bf16[64,64]{1,0:T(8,128)(2,1)S(1)} copy-done((bf16[64,64]{1,0:T(8,128)(2,1)S(1)}, bf16[64,64]{1,0:T(8,128)(2,1)}, u32[]{:S(2)}) %copy-start.5) | copy-done | bytes 8216
  6.8 59.7 %shard_map.73 = f32[2,48]{1,0:T(2,128)S(1)} custom-call(bf16[1,2,128,1024]{3,2,1,0:T(8,128)(2,1)S(1)} %copy-done.2, bf16[1,2,128,3072]{3,2,1,0:T(8,128)(2,1)S(1)} %copy-done, bf16[1,1,128,1024]{3,2,1,0:T(8,128)(2,1)S(1)} %copy-done.3, bf16[1,1,128,3072]{3,2,1,0:T(8,128)(2,1)S(1)} %copy-done.1, bf16[64,1024]{1,0:T(8,128)(2,1)S(1)} %copy-done.4, ...), custom_call_target="tpu_custom_call" | custom-call | tf_op jit(solution)/shard_map/pallas_call | solution.py:253
  66.5 0.6 copy.10
Async XLA Ops:
  0.7 1.4 %copy-start = (bf16[1,2,128,3072]{3,2,1,0:T(8,128)(2,1)S(1)}, bf16[1,2,128,3072]{3,2,1,0:T(8,128)(2,1)}, u32[]{:S(2)}) copy-start(bf16[1,2,128,3072]{3,2,1,0:T(8,128)(2,1)} %train_grads.1) | copy-start | bytes 4718596
  2.1 1.1 %copy-start.1 = (bf16[1,1,128,3072]{3,2,1,0:T(8,128)(2,1)S(1)}, bf16[1,1,128,3072]{3,2,1,0:T(8,128)(2,1)}, u32[]{:S(2)}) copy-start(bf16[1,1,128,3072]{3,2,1,0:T(8,128)(2,1)} %query_grads.1) | copy-start | bytes 2359300
  3.2 1.0 %copy-start.2 = (bf16[1,2,128,1024]{3,2,1,0:T(8,128)(2,1)S(1)}, bf16[1,2,128,1024]{3,2,1,0:T(8,128)(2,1)}, u32[]{:S(2)}) copy-start(bf16[1,2,128,1024]{3,2,1,0:T(8,128)(2,1)} %train_acts.1) | copy-start | bytes 1572868
  4.2 0.9 %copy-start.3 = (bf16[1,1,128,1024]{3,2,1,0:T(8,128)(2,1)S(1)}, bf16[1,1,128,1024]{3,2,1,0:T(8,128)(2,1)}, u32[]{:S(2)}) copy-start(bf16[1,1,128,1024]{3,2,1,0:T(8,128)(2,1)} %query_acts.1) | copy-start | bytes 786436
  5.2 0.9 %copy-start.4 = (bf16[64,1024]{1,0:T(8,128)(2,1)S(1)}, bf16[64,1024]{1,0:T(8,128)(2,1)}, u32[]{:S(2)}) copy-start(bf16[64,1024]{1,0:T(8,128)(2,1)} %proj_in.1) | copy-start | bytes 393220
  6.1 0.7 %copy-start.5 = (bf16[64,64]{1,0:T(8,128)(2,1)S(1)}, bf16[64,64]{1,0:T(8,128)(2,1)}, u32[]{:S(2)}) copy-start(bf16[64,64]{1,0:T(8,128)(2,1)} %proj_out.1) | copy-start | bytes 24580

commit v2 on v1

--- a/solution.py
+++ b/solution.py
@@ -24,30 +24,37 @@
     train_acts, train_grads, query_acts, query_grads, proj_in, proj_out, step,
     out,
     acts, grads, pin, pout, pbuf, at_part, at_recv, at_full, bsum, gp, grecv, zq, crow, dbuf,
-    load_sem, pz_recv, pr_recv, pl_recv, p_send, ring_send,
+    load_sem, pz_recv, py_recv, pz_send, py_send,
     a_send, a_recv, ag_send, ag_recv, g_send, g_recv, z_send, z_recv, y_send, y_recv, d_send, d_recv,
 ):
     ver = lax.axis_index("ver")
     fsdp = lax.axis_index("fsdp")
     tp = lax.axis_index("tp")
-    y, z = fsdp // NZ, fsdp % NZ
+    y, z = lax.div(fsdp, NZ), lax.rem(fsdp, NZ)
     half = NZ // 2
     trains, queries = train_acts.shape[1], query_acts.shape[1]
     count = trains + queries
     seq = train_acts.shape[2]
     tokens = count * seq
 
-    def at_z(d):
-        return {"fsdp": y * NZ + (z + d) % NZ}
+    def at_z(zz):
+        return {"fsdp": y * NZ + zz}
 
     def at_y(d):
-        return {"fsdp": ((y + d) % ny) * NZ + z}
+        return {"fsdp": lax.rem(y + d, ny) * NZ + z}
 
     def at_tp(d):
-        return {"tp": (tp + d) % ntp}
+        return {"tp": lax.rem(tp + d, ntp)}
 
     def at_ver(v, d):
-        return {"ver": (ver + v) % nver, "tp": (tp + d) % ntp}
+        return {"ver": lax.rem(ver + v, nver), "tp": lax.rem(tp + d, ntp)}
+
+    tp_order = sorted(range(1, ntp), key=lambda d: abs(d - ntp // 2))
+    y_order = sorted(range(1, ny), key=lambda d: abs(d - ny // 2))
+    ver_order = [(v, d) for v in range(1, nver) for d in tp_order + [0]]
+    zhalf, zpos = lax.div(z, half), lax.rem(z, half)
+    other_z = [(1 - zhalf) * half + j for j in range(half)]
+    same_z = [zhalf * half + lax.rem(zpos + i, half) for i in range(1, half)]
 
     def push(src, dst, send, recv, where):
         copy = pltpu.make_async_remote_copy(
@@ -61,8 +68,10 @@
     load_pout = pltpu.make_async_copy(proj_out, pout, load_sem.at[0])
     load_pout.start()
     barrier = pltpu.get_barrier_semaphore()
-    partners = [at_y(d) for d in range(1, ny)] + [at_z(d) for d in range(1, NZ)] + [at_tp(d) for d in range(1, ntp)]
-    partners += [at_ver(v, d) for v in range(1, nver) for d in range(ntp)]
+    partners = [at_ver(v, d) for v, d in ver_order]
+    partners += [at_y(d) for d in y_order[:1]] + [at_z(zz) for zz in other_z] + [at_y(d) for d in y_order[1:3]]
+    partners += [at_tp(d) for d in tp_order[:3]] + [at_y(d) for d in y_order[3:]] + [at_z(zz) for zz in same_z]
+    partners += [at_tp(d) for d in tp_order[3:]]
     for where in partners:
         pl.semaphore_signal(barrier, inc=1, device_id=where, device_id_type=MESH)
     loads_a = [
@@ -80,42 +89,39 @@
     load_pout.wait()
     own = pout[...].astype(F32)
     rank = own.shape[0]
-    pbuf[y, z] = jnp.concatenate([own[: rank // 2], own[rank // 2 :]], axis=1).astype(BF16)
+    pbuf[y, 0] = jnp.concatenate([own[: rank // 2], own[rank // 2 :]], axis=1).astype(BF16)
 
     pl.semaphore_wait(barrier, len(partners))
-    for d in range(1, NZ):
-        push(pbuf.at[y, z], pbuf.at[y, z], p_send, pz_recv.at[z], at_z(d))
+    pieces = (pl.ds(0, 1), pl.ds(1, half - 1), pl.ds(half, half))
+
+    def push_row(piece):
+        for d in y_order:
+            push(pbuf.at[y, piece], pbuf.at[y, piece], py_send, py_recv.at[d], at_y(d))
+
+    for zz in other_z:
+        push(pbuf.at[y, 0], pbuf.at[y, half + zpos], pz_send, pz_recv.at[1], at_z(zz))
+    for i, zz in enumerate(same_z):
+        push(pbuf.at[y, 0], pbuf.at[y, half - 1 - i], pz_send, pz_recv.at[0], at_z(zz))
+    push_row(pieces[0])
 
     for load in loads_a:
         load.wait()
     a_part = lax.dot_general(pin[...], acts[...].reshape(tokens, -1), NT, preferred_element_type=F32)
     at_part[...] = a_part.reshape(at_part.shape)
-    for d in range(1, ntp):
+    for d in tp_order:
         push(at_part.at[(tp + d) % ntp], at_recv.at[d - 1], a_send, a_recv, at_tp(d))
-
-    first = z // half
-    chunks = (first, 1 - first)
-    hops_right = (ny // 2, ny // 2 - 1)
-    hops_left = (ny // 2 - 1, ny // 2)
-
-    def send_right(s, k):
-        row = (y + ny - s) % ny
-        part = pbuf.at[row, pl.ds(chunks[k] * half, half)]
-        push(part, part, ring_send, pr_recv.at[s * 2 + k], at_y(1))
-
-    def send_left(s, k):
-        row = (y + s) % ny
-        part = pbuf.at[row, pl.ds(chunks[k] * half, half)]
-        push(part, part, ring_send, pl_recv.at[s * 2 + k], at_y(ny - 1))
 
     lane = lax.broadcasted_iota(jnp.int32, (rank // 2, 2 * rank), 1)
     is_left = lane < rank
+    slots = [
+        jnp.where(k // half == zhalf, lax.rem(k % half - zpos + half, half), half + k % half) for k in range(NZ)
+    ]
 
     def add_row(row, start):
         cols = []
         for p in range(half):
-            even = pbuf[row, 2 * p].astype(F32)
-            odd = pbuf[row, 2 * p + 1].astype(F32)
+            even = pbuf[row, slots[2 * p]].astype(F32)
+            odd = pbuf[row, slots[2 * p + 1]].astype(F32)
             low = jnp.where(is_left, even, pltpu.roll(odd, rank, 1)).astype(BF16)
             high = jnp.where(is_left, pltpu.roll(even, rank, 1), odd).astype(BF16)
             cols.append(jnp.concatenate([low, high, low, high], axis=0))
@@ -127,19 +133,9 @@
         else:
             bsum[...] += term
 
-    one_block = pbuf.at[0, 0]
-    one_chunk = pbuf.at[0, pl.ds(0, half)]
-    for k in range(2):
-        if k == 0:
-            others = [first * half + (z % half + i) % half for i in range(1, half)]
-        else:
-            others = [(1 - first) * half + i for i in range(half)]
-        for other in others:
-            wait(one_block, pz_recv.at[other])
-        if hops_right[k] > 0:
-            send_right(0, k)
-        if hops_left[k] > 0:
-            send_left(0, k)
+    for piece, sem in ((pieces[1], 0), (pieces[2], 1)):
+        wait(pbuf.at[y, piece], pz_recv.at[sem])
+        push_row(piece)
     for load in loads_g:
         load.wait()
     add_row(y, True)
@@ -149,22 +145,13 @@
     for d in range(ntp - 1):
         mine = mine + at_recv[d]
     at_full[tp] = mine
-    for d in range(1, ntp):
+    for d in tp_order:
         push(at_full.at[tp], at_full.at[tp], ag_send, ag_recv, at_tp(d))
 
-    for s in range(1, ny // 2 + 1):
-        for k in range(2):
-            if s - 1 < hops_right[k]:
-                wait(one_chunk, pr_recv.at[(s - 1) * 2 + k])
-                if s < hops_right[k]:
-                    send_right(s, k)
-            if s - 1 < hops_left[k]:
-                wait(one_chunk, pl_recv.at[(s - 1) * 2 + k])
-                if s < hops_left[k]:
-                    send_left(s, k)
-        add_row((y + ny - s) % ny, False)
-        if s < ny // 2:
-            add_row((y + s) % ny, False)
+    for d in reversed(y_order):
+        row = lax.rem(y + ny - d, ny)
+        wait(pbuf.at[row], py_recv.at[d])
+        add_row(row, False)
 
     wait(at_full.at[pl.ds(0, ntp - 1)], ag_recv)
     lanes2 = lax.broadcasted_iota(jnp.int32, (seq, 2 * rank), 1) < rank
@@ -178,7 +165,7 @@
         grad = both[: rank // 2] + (both[rank // 2 :] + jnp.dot(a_hi, b_lo, preferred_element_type=F32))
         for t in range(ntp):
             gp[t, n * rows : (n + 1) * rows, :] = grad[t * rows : (t + 1) * rows, :]
-    for d in range(1, ntp):
+    for d in tp_order:
         push(gp.at[(tp + d) % ntp], grecv.at[d - 1], g_send, g_recv, at_tp(d))
     wait(grecv, g_recv)
     grad = gp[tp]
@@ -186,12 +173,12 @@
         grad = grad + grecv[d]
 
     zq[z] = grad[trains * rows :, :]
-    for d in range(1, NZ):
-        push(zq.at[z], zq.at[z], z_send, z_recv, at_z(d))
+    for zz in other_z + same_z:
+        push(zq.at[z], zq.at[z], z_send, z_recv, at_z(zz))
     wait(zq.at[pl.ds(0, NZ - 1)], z_recv)
     for k in range(NZ):
         crow[y, k * rows : (k + 1) * rows, :] = zq[k]
-    for d in range(1, ny):
+    for d in y_order:
         push(crow.at[y], crow.at[y], y_send, y_recv, at_y(d))
     wait(crow.at[pl.ds(0, ny - 1)], y_recv)
 
@@ -215,10 +202,8 @@
     me = ver * ntp + tp
     dbuf[me] = part * (step[0] / (seq * seq))
 
-    for v in reversed(range(nver)):
-        for d in range(ntp):
-            if v or d:
-                push(dbuf.at[me], dbuf.at[me], d_send, d_recv, at_ver(v, d))
+    for v, d in ver_order + [(0, d) for d in tp_order]:
+        push(dbuf.at[me], dbuf.at[me], d_send, d_recv, at_ver(v, d))
     wait(dbuf.at[pl.ds(0, nver * ntp - 1)], d_recv)
     total = dbuf[0]
     for i in range(1, nver * ntp):
@@ -227,8 +212,8 @@
     for n in range(trains):
         out[n : n + 1, :] = jnp.sum(total[n * rows : (n + 1) * rows, :], axis=0, keepdims=True)[:, :width]
 
-    wait(pbuf.at[0, pl.ds(0, NZ - 1)], p_send)
-    wait(pbuf.at[pl.ds(0, ny - 1)], ring_send)
+    wait(pbuf.at[0, pl.ds(0, NZ - 1)], pz_send)
+    wait(pbuf.at[pl.ds(0, ny - 1)], py_send)
     wait(at_recv, a_send)
     wait(at_recv, ag_send)
     wait(grecv, g_send)
@@ -270,11 +255,11 @@
                 pltpu.VMEM((NZ, rows, 2 * rank), F32),
                 pltpu.VMEM((ny, NZ * rows, 2 * rank), F32),
                 pltpu.VMEM((nver * ntp, trains * rows, 128), F32),
-                dma((6,)), dma((NZ,)), dma((ny,)), dma((ny,)), dma, dma,
+                dma((6,)), dma((2,)), dma((ny,)), dma, dma,
                 dma, dma, dma, dma, dma, dma, dma, dma, dma, dma, dma, dma,
             ],
             compiler_params=pltpu.CompilerParams(
-                collective_id=0, has_side_effects=True, vmem_limit_bytes=40 * 1024 * 1024
+                collective_id=0, has_side_effects=True, vmem_limit_bytes=60 * 1024 * 1024
             ),
         )(train_acts, train_grads, query_acts, query_grads, proj_in, proj_out, step_sizes)
 

time: 67.4 us -> 56.6 us (0.84)
  local copies, waits for them, and re-layouts: 6.71 us -> 1.24 us
  Pallas kernels: 59.7 us -> 54.5 us
    unnamed x13 -> x1, local copies, waits for them, and re-layouts: 6.71 us -> 1.24 us
    pallas_call x1, Pallas kernels: 59.7 us -> 54.5 us  [body(): pl.pallas_call(functools.partial(kernel, nver, ny, ntp), out_shape=jax.Sh...]
where the time goes in v2:
time: 56.6 us; the launch traced here: 56.4 us
  Pallas kernels  54.5 us (96%)
  local copies, waits for them, and re-layouts  1.24 us (2%)
  between operations  0.66 us (1%)
    pallas_call x1, Pallas kernels, body(): pl.pallas_call(functools.partial(kernel, nver, ny, ntp), out_shape=jax.Sh...  54.5 us
    unnamed x1, local copies, waits for them, and re-layouts  1.24 us

profile of v2, /device:TPU:1, one launch (start us, length us, event | category | flops | bytes accessed | tf_op | source)
XLA Modules:
  0.0 56.4 jit_solution(6566592835501123779)
XLA Ops:
  0.7 54.5 %shard_map.73 = f32[2,48]{1,0:T(2,128)} custom-call(bf16[1,2,128,1024]{3,2,1,0:T(8,128)(2,1)} %train_acts.1, bf16[1,2,128,3072]{3,2,1,0:T(8,128)(2,1)} %train_grads.1, bf16[1,1,128,1024]{3,2,1,0:T(8,128)(2,1)} %query_acts.1, bf16[1,1,128,3072]{3,2,1,0:T(8,128)(2,1)} %query_grads.1, bf16[64,1024]{1,0:T(8,128)(2,1)} %proj_in.1, bf16[64,64]{1,0:T(8,128)(2,1)} %proj_out.1, ...), custom_call_target="tpu_custom_call" | custom-call | tf_op jit(solution)/shard_map/pallas_call | solution.py:238
  55.2 1.2 %copy.10 = f32[2,48]{1,0:T(2,128)} copy(f32[2,48]{1,0:T(2,128)} %shard_map.73) | data formatting | bytes 768

commit v3 on v2

--- a/solution.py
+++ b/solution.py
@@ -21,11 +21,11 @@
 
 def kernel(
     nver, ny, ntp,
-    train_acts, train_grads, query_acts, query_grads, proj_in, proj_out, step,
+    train_acts, train_grads, query_acts, query_grads, proj_in, proj_out, step_size,
     out,
-    acts, grads, pin, pout, pbuf, at_part, at_recv, at_full, bsum, gp, grecv, zq, crow, dbuf,
-    load_sem, pz_recv, py_recv, pz_send, py_send,
-    a_send, a_recv, ag_send, ag_recv, g_send, g_recv, z_send, z_recv, y_send, y_recv, d_send, d_recv,
+    acts, grads, pin, pout, pbuf, at_part, at_recv, at_full, bsum, gp, grecv, qbuf, crow, dbuf, step,
+    load_sem, p_sems, p_far, q_sems, q_far,
+    a_send, a_recv, ag_send, ag_recv, g_send, g_recv, d_send, d_recv,
 ):
     ver = lax.axis_index("ver")
     fsdp = lax.axis_index("fsdp")
@@ -68,10 +68,9 @@
     load_pout = pltpu.make_async_copy(proj_out, pout, load_sem.at[0])
     load_pout.start()
     barrier = pltpu.get_barrier_semaphore()
-    partners = [at_ver(v, d) for v, d in ver_order]
-    partners += [at_y(d) for d in y_order[:1]] + [at_z(zz) for zz in other_z] + [at_y(d) for d in y_order[1:3]]
-    partners += [at_tp(d) for d in tp_order[:3]] + [at_y(d) for d in y_order[3:]] + [at_z(zz) for zz in same_z]
-    partners += [at_tp(d) for d in tp_order[3:]]
+    partners = [at_z(zz) for zz in other_z] + [at_y(d) for d in y_order[:3]]
+    partners += [at_ver(v, d) for v, d in ver_order] + [at_tp(d) for d in tp_order[:3]]
+    partners += [at_y(d) for d in y_order[3:]] + [at_z(zz) for zz in same_z] + [at_tp(d) for d in tp_order[3:]]
     for where in partners:
         pl.semaphore_signal(barrier, inc=1, device_id=where, device_id_type=MESH)
     loads_a = [
@@ -83,39 +82,53 @@
         pltpu.make_async_copy(train_grads.at[0], grads.at[pl.ds(0, trains)], load_sem.at[4]),
         pltpu.make_async_copy(query_grads.at[0], grads.at[pl.ds(trains, queries)], load_sem.at[5]),
     ]
-    for load in loads_a + loads_g:
+    load_step = pltpu.make_async_copy(step_size, step, load_sem.at[6])
+    for load in loads_a + loads_g + [load_step]:
         load.start()
+
+    near, far = pl.ds(1, half - 1), pl.ds(half, half)
+
+    def gather_own(buf, sems):
+        for zz in other_z:
+            push(buf.at[y, 0], buf.at[y, half + zpos], sems.at[0], sems.at[4], at_z(zz))
+        for d in y_order:
+            push(buf.at[y, 0], buf.at[y, 0], sems.at[1], sems.at[5], at_y(d))
+
+    def gather_rest(buf, sems, far_recv):
+        wait(buf.at[y, far], sems.at[4])
+        for d in y_order:
+            push(buf.at[y, far], buf.at[y, far], sems.at[3], far_recv.at[d], at_y(d))
+        wait(buf.at[pl.ds(0, ny - 1), 0], sems.at[5])
+        for i, zz in enumerate(same_z):
+            push(buf.at[:, 0], buf.at[:, half - 1 - i], sems.at[2], sems.at[6], at_z(zz))
+
+    def gather_sent(buf, sems):
+        wait(buf.at[0, far], sems.at[0])
+        wait(buf.at[pl.ds(0, ny - 1), 0], sems.at[1])
+        wait(buf.at[:, near], sems.at[2])
+        wait(buf.at[pl.ds(0, ny - 1), far], sems.at[3])
+
+    slots = [
+        jnp.where(k // half == zhalf, lax.rem(k % half - zpos + half, half), half + k % half) for k in range(NZ)
+    ]
 
     load_pout.wait()
     own = pout[...].astype(F32)
     rank = own.shape[0]
     pbuf[y, 0] = jnp.concatenate([own[: rank // 2], own[rank // 2 :]], axis=1).astype(BF16)
 
-    pl.semaphore_wait(barrier, len(partners))
-    pieces = (pl.ds(0, 1), pl.ds(1, half - 1), pl.ds(half, half))
-
-    def push_row(piece):
-        for d in y_order:
-            push(pbuf.at[y, piece], pbuf.at[y, piece], py_send, py_recv.at[d], at_y(d))
-
-    for zz in other_z:
-        push(pbuf.at[y, 0], pbuf.at[y, half + zpos], pz_send, pz_recv.at[1], at_z(zz))
-    for i, zz in enumerate(same_z):
-        push(pbuf.at[y, 0], pbuf.at[y, half - 1 - i], pz_send, pz_recv.at[0], at_z(zz))
-    push_row(pieces[0])
-
     for load in loads_a:
         load.wait()
     a_part = lax.dot_general(pin[...], acts[...].reshape(tokens, -1), NT, preferred_element_type=F32)
     at_part[...] = a_part.reshape(at_part.shape)
+    pl.semaphore_wait(barrier, len(partners))
+    gather_own(pbuf, p_sems)
+
     for d in tp_order:
         push(at_part.at[(tp + d) % ntp], at_recv.at[d - 1], a_send, a_recv, at_tp(d))
 
     lane = lax.broadcasted_iota(jnp.int32, (rank // 2, 2 * rank), 1)
     is_left = lane < rank
-    slots = [
-        jnp.where(k // half == zhalf, lax.rem(k % half - zpos + half, half), half + k % half) for k in range(NZ)
-    ]
 
     def add_row(row, start):
         cols = []
@@ -133,13 +146,9 @@
         else:
             bsum[...] += term
 
-    for piece, sem in ((pieces[1], 0), (pieces[2], 1)):
-        wait(pbuf.at[y, piece], pz_recv.at[sem])
-        push_row(piece)
-    for load in loads_g:
+    gather_rest(pbuf, p_sems, p_far)
+    for load in loads_g + [load_step]:
         load.wait()
-    add_row(y, True)
-
     wait(at_recv, a_recv)
     mine = at_part[tp]
     for d in range(ntp - 1):
@@ -148,9 +157,11 @@
     for d in tp_order:
         push(at_full.at[tp], at_full.at[tp], ag_send, ag_recv, at_tp(d))
 
+    wait(pbuf.at[:, near], p_sems.at[6])
+    add_row(y, True)
     for d in reversed(y_order):
         row = lax.rem(y + ny - d, ny)
-        wait(pbuf.at[row], py_recv.at[d])
+        wait(pbuf.at[row, far], p_far.at[d])
         add_row(row, False)
 
     wait(at_full.at[pl.ds(0, ntp - 1)], ag_recv)
@@ -172,15 +183,16 @@
     for d in range(ntp - 1):
         grad = grad + grecv[d]
 
-    zq[z] = grad[trains * rows :, :]
-    for zz in other_z + same_z:
-        push(zq.at[z], zq.at[z], z_send, z_recv, at_z(zz))
-    wait(zq.at[pl.ds(0, NZ - 1)], z_recv)
-    for k in range(NZ):
-        crow[y, k * rows : (k + 1) * rows, :] = zq[k]
-    for d in y_order:
-        push(crow.at[y], crow.at[y], y_send, y_recv, at_y(d))
-    wait(crow.at[pl.ds(0, ny - 1)], y_recv)
+    qbuf[y, 0] = grad[trains * rows :, :]
+    gather_own(qbuf, q_sems)
+    gather_rest(qbuf, q_sems, q_far)
+    wait(qbuf.at[:, near], q_sems.at[6])
+    for d in [0] + y_order[::-1]:
+        row = lax.rem(y + ny - d, ny)
+        if d:
+            wait(qbuf.at[row, far], q_far.at[d])
+        for k in range(NZ):
+            crow[row, k * rows : (k + 1) * rows, :] = qbuf[row, slots[k]]
 
     wide = ny * NZ * rows
     q_hi, q_lo = split(crow[...].reshape(wide, 2 * rank))
@@ -202,8 +214,10 @@
     me = ver * ntp + tp
     dbuf[me] = part * (step[0] / (seq * seq))
 
-    for v, d in ver_order + [(0, d) for d in tp_order]:
-        push(dbuf.at[me], dbuf.at[me], d_send, d_recv, at_ver(v, d))
+    targets = [{"ver": 0, "tp": lax.rem(tp + d, ntp)} for d in tp_order] + [at_ver(v, 0) for v in range(1, nver)]
+    targets += [{"ver": v, "tp": lax.rem(tp + d, ntp)} for v in range(1, nver) for d in tp_order]
+    for where in targets:
+        push(dbuf.at[me], dbuf.at[me], d_send, d_recv, where)
     wait(dbuf.at[pl.ds(0, nver * ntp - 1)], d_recv)
     total = dbuf[0]
     for i in range(1, nver * ntp):
@@ -212,13 +226,11 @@
     for n in range(trains):
         out[n : n + 1, :] = jnp.sum(total[n * rows : (n + 1) * rows, :], axis=0, keepdims=True)[:, :width]
 
-    wait(pbuf.at[0, pl.ds(0, NZ - 1)], pz_send)
-    wait(pbuf.at[pl.ds(0, ny - 1)], py_send)
+    gather_sent(pbuf, p_sems)
+    gather_sent(qbuf, q_sems)
     wait(at_recv, a_send)
     wait(at_recv, ag_send)
     wait(grecv, g_send)
-    wait(zq.at[pl.ds(0, NZ - 1)], z_send)
-    wait(crow.at[pl.ds(0, ny - 1)], y_send)
     wait(dbuf.at[pl.ds(0, nver * ntp - 1)], d_send)
 
 
@@ -238,7 +250,7 @@
         return pl.pallas_call(
             functools.partial(kernel, nver, ny, ntp),
             out_shape=jax.ShapeDtypeStruct((trains, nfsdp * queries), F32),
-            in_specs=[hbm] * 6 + [pl.BlockSpec(memory_space=pltpu.SMEM)],
+            in_specs=[hbm] * 7,
             out_specs=pl.BlockSpec(memory_space=pltpu.VMEM),
             scratch_shapes=[
                 pltpu.VMEM((count, seq, din), BF16),
@@ -252,14 +264,15 @@
                 pltpu.VMEM((tokens, 2 * rank), F32),
                 pltpu.VMEM((ntp, count * rows, 2 * rank), F32),
                 pltpu.VMEM((ntp - 1, count * rows, 2 * rank), F32),
-                pltpu.VMEM((NZ, rows, 2 * rank), F32),
+                pltpu.VMEM((ny, NZ, rows, 2 * rank), F32),
                 pltpu.VMEM((ny, NZ * rows, 2 * rank), F32),
                 pltpu.VMEM((nver * ntp, trains * rows, 128), F32),
-                dma((6,)), dma((2,)), dma((ny,)), dma, dma,
-                dma, dma, dma, dma, dma, dma, dma, dma, dma, dma, dma, dma,
+                pltpu.SMEM((1,), F32),
+                dma((7,)), dma((7,)), dma((ny,)), dma((7,)), dma((ny,)),
+                dma, dma, dma, dma, dma, dma, dma, dma,
             ],
             compiler_params=pltpu.CompilerParams(
-                collective_id=0, has_side_effects=True, vmem_limit_bytes=60 * 1024 * 1024
+                collective_id=0, has_side_effects=True, vmem_limit_bytes=56550000
             ),
         )(train_acts, train_grads, query_acts, query_grads, proj_in, proj_out, step_sizes)
 

time: 56.6 us -> 54.6 us (0.965)
  Pallas kernels: 54.5 us -> 53.2 us
  local copies, waits for them, and re-layouts: 1.24 us -> 0.56 us
    pallas_call x1, Pallas kernels: 54.5 us -> 53.2 us  [body(): pl.pallas_call(functools.partial(kernel, nver, ny, ntp), out_shape=jax.Sh...]
    unnamed x1, local copies, waits for them, and re-layouts: 1.24 us -> 0.56 us
where the time goes in v3:
time: 54.6 us; the launch traced here: 54.5 us
  Pallas kernels  53.2 us (97%)
  between operations  0.66 us (1%)
  local copies, waits for them, and re-layouts  0.56 us (1%)
    pallas_call x1, Pallas kernels, body(): pl.pallas_call(functools.partial(kernel, nver, ny, ntp), out_shape=jax.Sh...  53.2 us

profile of v3, /device:TPU:1, one launch (start us, length us, event | category | flops | bytes accessed | tf_op | source)
XLA Modules:
  0.0 54.5 jit_solution(3774081774995645556)
XLA Ops:
  0.7 53.2 %shard_map.73 = f32[2,48]{1,0:T(2,128)S(1)} custom-call(bf16[1,2,128,1024]{3,2,1,0:T(8,128)(2,1)} %train_acts.1, bf16[1,2,128,3072]{3,2,1,0:T(8,128)(2,1)} %train_grads.1, bf16[1,1,128,1024]{3,2,1,0:T(8,128)(2,1)} %query_acts.1, bf16[1,1,128,3072]{3,2,1,0:T(8,128)(2,1)} %query_grads.1, bf16[64,1024]{1,0:T(8,128)(2,1)} %proj_in.1, bf16[64,64]{1,0:T(8,128)(2,1)} %proj_out.1, ...), custom_call_target="tpu_custom_call" | custom-call | tf_op jit(solution)/shard_map/pallas_call | solution.py:250
  53.9 0.6 %copy.10 = f32[2,48]{1,0:T(2,128)} copy(f32[2,48]{1,0:T(2,128)S(1)} %shard_map.73) | data formatting | bytes 768

commit v4 on v3

--- a/solution.py
+++ b/solution.py
@@ -23,9 +23,9 @@
     nver, ny, ntp,
     train_acts, train_grads, query_acts, query_grads, proj_in, proj_out, step_size,
     out,
-    acts, grads, pin, pout, pbuf, at_part, at_recv, at_full, bsum, gp, grecv, qbuf, crow, dbuf, step,
+    acts, grads, pin, pout, pbuf, at_part, at_recv, at_full, pfull, bsum, gp, grecv, gq, gqrecv, qbuf, crow, dbuf, step,
     load_sem, p_sems, p_far, q_sems, q_far,
-    a_send, a_recv, ag_send, ag_recv, g_send, g_recv, d_send, d_recv,
+    a_send, a_recv, ag_send, ag_recv, g_send, g_recv, gq_send, gq_recv, d_send, d_recv,
 ):
     ver = lax.axis_index("ver")
     fsdp = lax.axis_index("fsdp")
@@ -87,26 +87,31 @@
         load.start()
 
     near, far = pl.ds(1, half - 1), pl.ds(half, half)
-
-    def gather_own(buf, sems):
+    opposite = lax.rem(y + ny // 2, ny)
+
+    def gather_own(buf, sems, far_recv):
         for zz in other_z:
             push(buf.at[y, 0], buf.at[y, half + zpos], sems.at[0], sems.at[4], at_z(zz))
         for d in y_order:
-            push(buf.at[y, 0], buf.at[y, 0], sems.at[1], sems.at[5], at_y(d))
+            recv = far_recv.at[0] if d == y_order[0] else sems.at[5]
+            push(buf.at[y, 0], buf.at[y, 0], sems.at[1], recv, at_y(d))
 
     def gather_rest(buf, sems, far_recv):
-        wait(buf.at[y, far], sems.at[4])
-        for d in y_order:
-            push(buf.at[y, far], buf.at[y, far], sems.at[3], far_recv.at[d], at_y(d))
-        wait(buf.at[pl.ds(0, ny - 1), 0], sems.at[5])
+        wait(buf.at[opposite, 0], far_recv.at[0])
+        for zz in other_z:
+            push(buf.at[opposite, 0], buf.at[opposite, half + zpos], sems.at[0], far_recv.at[y_order[0]], at_z(zz))
+        wait(buf.at[pl.ds(0, ny - 2), 0], sems.at[5])
         for i, zz in enumerate(same_z):
             push(buf.at[:, 0], buf.at[:, half - 1 - i], sems.at[2], sems.at[6], at_z(zz))
+        wait(buf.at[y, far], sems.at[4])
+        for d in y_order[1:]:
+            push(buf.at[y, far], buf.at[y, far], sems.at[3], far_recv.at[d], at_y(d))
 
     def gather_sent(buf, sems):
-        wait(buf.at[0, far], sems.at[0])
+        wait(buf.at[pl.ds(0, 2), far], sems.at[0])
         wait(buf.at[pl.ds(0, ny - 1), 0], sems.at[1])
         wait(buf.at[:, near], sems.at[2])
-        wait(buf.at[pl.ds(0, ny - 1), far], sems.at[3])
+        wait(buf.at[pl.ds(0, ny - 2), far], sems.at[3])
 
     slots = [
         jnp.where(k // half == zhalf, lax.rem(k % half - zpos + half, half), half + k % half) for k in range(NZ)
@@ -122,7 +127,7 @@
     a_part = lax.dot_general(pin[...], acts[...].reshape(tokens, -1), NT, preferred_element_type=F32)
     at_part[...] = a_part.reshape(at_part.shape)
     pl.semaphore_wait(barrier, len(partners))
-    gather_own(pbuf, p_sems)
+    gather_own(pbuf, p_sems, p_far)
 
     for d in tp_order:
         push(at_part.at[(tp + d) % ntp], at_recv.at[d - 1], a_send, a_recv, at_tp(d))
@@ -139,12 +144,14 @@
             high = jnp.where(is_left, pltpu.roll(even, rank, 1), odd).astype(BF16)
             cols.append(jnp.concatenate([low, high, low, high], axis=0))
         width = NZ * rank
-        g = grads[:, :, pl.ds(pl.multiple_of(row * width, 128), width)].reshape(tokens, width)
-        term = lax.dot_general(g, jnp.concatenate(cols, axis=1), NT, preferred_element_type=F32)
+        columns = pl.ds(pl.multiple_of(row * width, 128), width)
+        pfull[:, columns] = jnp.concatenate(cols, axis=1)
+        g = grads[trains:, :, columns].reshape(queries * seq, width)
+        term = lax.dot_general(g, pfull[:, columns], NT, preferred_element_type=F32)
         if start:
-            bsum[...] = term
+            bsum[trains * seq :, :] = term
         else:
-            bsum[...] += term
+            bsum[trains * seq :, :] += term
 
     gather_rest(pbuf, p_sems, p_far)
     for load in loads_g + [load_step]:
@@ -167,7 +174,8 @@
     wait(at_full.at[pl.ds(0, ntp - 1)], ag_recv)
     lanes2 = lax.broadcasted_iota(jnp.int32, (seq, 2 * rank), 1) < rank
     rows = rank // 2 // ntp
-    for n in range(count):
+
+    def grad_parts(n, parts, at_row):
         at = at_full[:, :, n * seq : (n + 1) * seq].reshape(rank, seq)
         a_hi, a_lo = split(jnp.concatenate([at[: rank // 2], at[rank // 2 :]], axis=1))
         b = bsum[n * seq : (n + 1) * seq, :]
@@ -175,17 +183,29 @@
         both = jnp.dot(jnp.concatenate([a_hi, a_lo], axis=0), b_hi, preferred_element_type=F32)
         grad = both[: rank // 2] + (both[rank // 2 :] + jnp.dot(a_hi, b_lo, preferred_element_type=F32))
         for t in range(ntp):
-            gp[t, n * rows : (n + 1) * rows, :] = grad[t * rows : (t + 1) * rows, :]
+            parts[t, at_row : at_row + rows, :] = grad[t * rows : (t + 1) * rows, :]
+
+    grad_parts(trains, gq, 0)
     for d in tp_order:
-        push(gp.at[(tp + d) % ntp], grecv.at[d - 1], g_send, g_recv, at_tp(d))
+        push(gq.at[lax.rem(tp + d, ntp)], gqrecv.at[d - 1], gq_send, gq_recv, at_tp(d))
+    g = grads[:trains].reshape(trains * seq, -1)
+    bsum[: trains * seq, :] = lax.dot_general(g, pfull[...], NT, preferred_element_type=F32)
+    for n in range(trains):
+        grad_parts(n, gp, n * rows)
+    for d in tp_order:
+        push(gp.at[lax.rem(tp + d, ntp)], grecv.at[d - 1], g_send, g_recv, at_tp(d))
+    wait(gqrecv, gq_recv)
+    query = gq[tp]
+    for d in range(ntp - 1):
+        query = query + gqrecv[d]
+
+    qbuf[y, 0] = query
+    gather_own(qbuf, q_sems, q_far)
+    gather_rest(qbuf, q_sems, q_far)
     wait(grecv, g_recv)
     grad = gp[tp]
     for d in range(ntp - 1):
         grad = grad + grecv[d]
-
-    qbuf[y, 0] = grad[trains * rows :, :]
-    gather_own(qbuf, q_sems)
-    gather_rest(qbuf, q_sems, q_far)
     wait(qbuf.at[:, near], q_sems.at[6])
     for d in [0] + y_order[::-1]:
         row = lax.rem(y + ny - d, ny)
@@ -196,7 +216,7 @@
 
     wide = ny * NZ * rows
     q_hi, q_lo = split(crow[...].reshape(wide, 2 * rank))
-    t_hi, t_lo = split(grad[: trains * rows, :])
+    t_hi, t_lo = split(grad)
     many = trains * rows
     both = lax.dot_general(jnp.concatenate([t_hi, t_lo], axis=0), q_hi, NT, preferred_element_type=F32)
     cross = both[:many] + (both[many:] + lax.dot_general(t_hi, q_lo, NT, preferred_element_type=F32))
@@ -231,6 +251,7 @@
     wait(at_recv, a_send)
     wait(at_recv, ag_send)
     wait(grecv, g_send)
+    wait(gqrecv, gq_send)
     wait(dbuf.at[pl.ds(0, nver * ntp - 1)], d_send)
 
 
@@ -261,15 +282,18 @@
                 pltpu.VMEM((ntp, arows, tokens), F32),
                 pltpu.VMEM((ntp - 1, arows, tokens), F32),
                 pltpu.VMEM((ntp, arows, tokens), F32),
+                pltpu.VMEM((2 * rank, dout), BF16),
                 pltpu.VMEM((tokens, 2 * rank), F32),
-                pltpu.VMEM((ntp, count * rows, 2 * rank), F32),
-                pltpu.VMEM((ntp - 1, count * rows, 2 * rank), F32),
+                pltpu.VMEM((ntp, trains * rows, 2 * rank), F32),
+                pltpu.VMEM((ntp - 1, trains * rows, 2 * rank), F32),
+                pltpu.VMEM((ntp, queries * rows, 2 * rank), F32),
+                pltpu.VMEM((ntp - 1, queries * rows, 2 * rank), F32),
                 pltpu.VMEM((ny, NZ, rows, 2 * rank), F32),
                 pltpu.VMEM((ny, NZ * rows, 2 * rank), F32),
                 pltpu.VMEM((nver * ntp, trains * rows, 128), F32),
                 pltpu.SMEM((1,), F32),
                 dma((7,)), dma((7,)), dma((ny,)), dma((7,)), dma((ny,)),
-                dma, dma, dma, dma, dma, dma, dma, dma,
+                dma, dma, dma, dma, dma, dma, dma, dma, dma, dma,
             ],
             compiler_params=pltpu.CompilerParams(
                 collective_id=0, has_side_effects=True, vmem_limit_bytes=56550000

time: 54.6 us -> 53.6 us (0.982)
  Pallas kernels: 53.2 us -> 52.1 us
    pallas_call x1, Pallas kernels: 53.2 us -> 52.1 us  [body(): pl.pallas_call(functools.partial(kernel, nver, ny, ntp), out_shape=jax.Sh...]
where the time goes in v4:
time: 53.6 us; the launch traced here: 53.4 us
  Pallas kernels  52.1 us (97%)
  between operations  0.66 us (1%)
  local copies, waits for them, and re-layouts  0.56 us (1%)
    pallas_call x1, Pallas kernels, body(): pl.pallas_call(functools.partial(kernel, nver, ny, ntp), out_shape=jax.Sh...  52.1 us

profile of v4, /device:TPU:1, one launch (start us, length us, event | category | flops | bytes accessed | tf_op | source)
XLA Modules:
  0.0 53.4 jit_solution(7831179655098273625)
XLA Ops:
  0.7 52.1 %shard_map.73 = f32[2,48]{1,0:T(2,128)S(1)} custom-call(bf16[1,2,128,1024]{3,2,1,0:T(8,128)(2,1)} %train_acts.1, bf16[1,2,128,3072]{3,2,1,0:T(8,128)(2,1)} %train_grads.1, bf16[1,1,128,1024]{3,2,1,0:T(8,128)(2,1)} %query_acts.1, bf16[1,1,128,3072]{3,2,1,0:T(8,128)(2,1)} %query_grads.1, bf16[64,1024]{1,0:T(8,128)(2,1)} %proj_in.1, bf16[64,64]{1,0:T(8,128)(2,1)} %proj_out.1, ...), custom_call_target="tpu_custom_call" | custom-call | tf_op jit(solution)/shard_map/pallas_call | solution.py:271
  52.8 0.6 %copy.10 = f32[2,48]{1,0:T(2,128)} copy(f32[2,48]{1,0:T(2,128)S(1)} %shard_map.73) | data formatting | bytes 768

commit v5 on v4

--- a/solution.py
+++ b/solution.py
@@ -90,11 +90,11 @@
     opposite = lax.rem(y + ny // 2, ny)
 
     def gather_own(buf, sems, far_recv):
+        push(buf.at[y, 0], buf.at[y, 0], sems.at[1], far_recv.at[0], at_y(y_order[0]))
         for zz in other_z:
             push(buf.at[y, 0], buf.at[y, half + zpos], sems.at[0], sems.at[4], at_z(zz))
-        for d in y_order:
-            recv = far_recv.at[0] if d == y_order[0] else sems.at[5]
-            push(buf.at[y, 0], buf.at[y, 0], sems.at[1], recv, at_y(d))
+        for d in y_order[1:]:
+            push(buf.at[y, 0], buf.at[y, 0], sems.at[1], sems.at[5], at_y(d))
 
     def gather_rest(buf, sems, far_recv):
         wait(buf.at[opposite, 0], far_recv.at[0])
@@ -135,7 +135,7 @@
     lane = lax.broadcasted_iota(jnp.int32, (rank // 2, 2 * rank), 1)
     is_left = lane < rank
 
-    def add_row(row, start):
+    def place_row(row):
         cols = []
         for p in range(half):
             even = pbuf[row, slots[2 * p]].astype(F32)
@@ -146,12 +146,6 @@
         width = NZ * rank
         columns = pl.ds(pl.multiple_of(row * width, 128), width)
         pfull[:, columns] = jnp.concatenate(cols, axis=1)
-        g = grads[trains:, :, columns].reshape(queries * seq, width)
-        term = lax.dot_general(g, pfull[:, columns], NT, preferred_element_type=F32)
-        if start:
-            bsum[trains * seq :, :] = term
-        else:
-            bsum[trains * seq :, :] += term
 
     gather_rest(pbuf, p_sems, p_far)
     for load in loads_g + [load_step]:
@@ -165,11 +159,13 @@
         push(at_full.at[tp], at_full.at[tp], ag_send, ag_recv, at_tp(d))
 
     wait(pbuf.at[:, near], p_sems.at[6])
-    add_row(y, True)
+    place_row(y)
     for d in reversed(y_order):
         row = lax.rem(y + ny - d, ny)
         wait(pbuf.at[row, far], p_far.at[d])
-        add_row(row, False)
+        place_row(row)
+    g = grads[trains:].reshape(queries * seq, -1)
+    bsum[trains * seq :, :] = lax.dot_general(g, pfull[...], NT, preferred_element_type=F32)
 
     wait(at_full.at[pl.ds(0, ntp - 1)], ag_recv)
     lanes2 = lax.broadcasted_iota(jnp.int32, (seq, 2 * rank), 1) < rank

time: 53.6 us -> 52.7 us (0.983)
  Pallas kernels: 52.1 us -> 51.3 us
    pallas_call x1, Pallas kernels: 52.1 us -> 51.3 us  [body(): pl.pallas_call(functools.partial(kernel, nver, ny, ntp), out_shape=jax.Sh...]
where the time goes in v5:
time: 52.7 us; the launch traced here: 52.5 us
  Pallas kernels  51.3 us (97%)
  between operations  0.66 us (1%)
  local copies, waits for them, and re-layouts  0.56 us (1%)
    pallas_call x1, Pallas kernels, body(): pl.pallas_call(functools.partial(kernel, nver, ny, ntp), out_shape=jax.Sh...  51.3 us

profile of v5, /device:TPU:1, one launch (start us, length us, event | category | flops | bytes accessed | tf_op | source)
XLA Modules:
  0.0 52.5 jit_solution(1973106298211125044)
XLA Ops:
  0.7 51.3 %shard_map.73 = f32[2,48]{1,0:T(2,128)S(1)} custom-call(bf16[1,2,128,1024]{3,2,1,0:T(8,128)(2,1)} %train_acts.1, bf16[1,2,128,3072]{3,2,1,0:T(8,128)(2,1)} %train_grads.1, bf16[1,1,128,1024]{3,2,1,0:T(8,128)(2,1)} %query_acts.1, bf16[1,1,128,3072]{3,2,1,0:T(8,128)(2,1)} %query_grads.1, bf16[64,1024]{1,0:T(8,128)(2,1)} %proj_in.1, bf16[64,64]{1,0:T(8,128)(2,1)} %proj_out.1, ...), custom_call_target="tpu_custom_call" | custom-call | tf_op jit(solution)/shard_map/pallas_call | solution.py:267
  52.0 0.6 %copy.10 = f32[2,48]{1,0:T(2,128)} copy(f32[2,48]{1,0:T(2,128)S(1)} %shard_map.73) | data formatting | bytes 768
